TPU v7x, 32 devices: a whole 2x2x4 slice. The times are simulated.
32 devices in a mesh: grp: 4 (over y, x), mem: 8 (over z, core).
Axes of the slice: x: 2, y: 2, z: 4, core: 2. Of those that a mesh axis runs over, the one named last changes fastest.
Arguments:
- images: bfloat16 [1024, 18432], P(('grp', 'mem')), may hold values from -24 to 24
- classes: int32 [1024], P(('grp', 'mem')), may hold values from 0 to 199, as said below
- rotations: int32 [1024], P(('grp', 'mem')), may hold values from 0 to 35
- bins: int32 [1024], P(('grp', 'mem')), may hold values from 0 to 15
- ctf_table: float32 [16, 18432], replicated, may hold values from -1 to 1
Outputs:
- averages: float32 [200, 18432], P('grp', 'mem')
Inputs may be any that keep to these rules, and one draw needn't show every extreme that they name: The owner of a class c is c // 50. In each aligned block of 32 particles (one device's), at most 16 particles belong to classes of one owner, and exactly 16 do for some owner in every block.
All inputs are finite; a program needn't handle non-finite values.
Results may differ from a plain program's by a relative error of at most 0.0003.
Values may be sent and summed in bfloat16 or wider, within the bound.
No kernel may reach another device: no remote copies, remote signals or barrier semaphores. Data moves between devices by JAX's collectives and lax.ppermute only.
A program may use at most 256 MiB of HBM per device.

v0:
```python
import jax
import jax.numpy as jnp
from jax import lax
from jax.sharding import PartitionSpec as P

ANGLES = 144
ROTS = 36
BINS = 16
CPG = 50
SHIFT = 4
wiener_term = 1.0


def rotate(values, turns):
    count = values.shape[0]
    shaped = values.reshape(count, -1, ANGLES)
    levels = max(ROTS - 1, 1).bit_length()
    for level in range(levels):
        amount = SHIFT * (1 << level) % ANGLES
        rolled = jnp.concatenate([shaped[:, :, amount:], shaped[:, :, :amount]], axis=2)
        chosen = turns >> level & 1 == 1
        shaped = jnp.where(chosen[:, None, None], rolled, shaped)
    return shaped.reshape(count, -1)


def on_device(images, classes, rotations, bins, ctf_table):
    arrived = lax.all_to_all(images, "mem", split_axis=1, concat_axis=0, tiled=True)
    span = arrived.shape[1]
    labels = jnp.stack([classes, bins, rotations], axis=1)
    tags = lax.all_gather(labels, "mem", axis=0, tiled=True)
    class_here = tags[:, 0]
    bin_here = tags[:, 1]
    turn_here = tags[:, 2]
    member = (
        jnp.arange(CPG * lax.axis_size("grp"), dtype=jnp.int32)[:, None] == class_here[None, :]
    ).astype(jnp.float32)
    bin_pick = (bin_here[:, None] == jnp.arange(BINS, dtype=jnp.int32)[None, :]).astype(jnp.float32)
    ctf_slice = lax.dynamic_slice_in_dim(ctf_table, lax.axis_index("mem") * span, span, 1)
    ctf_rows = jnp.dot(bin_pick, ctf_slice, precision=lax.Precision.HIGHEST)
    aligned = rotate(ctf_rows * arrived.astype(jnp.float32), turn_here)
    numer = jnp.dot(member, aligned, precision=lax.Precision.HIGHEST)
    weights = rotate(ctf_rows * ctf_rows, turn_here)
    denom_part = jnp.dot(member, weights, precision=lax.Precision.HIGHEST)
    numer_here, denom_here = (
        lax.psum_scatter(numer, "grp", scatter_dimension=0, tiled=True),
        lax.psum_scatter(denom_part, "grp", scatter_dimension=0, tiled=True),
    )
    return numer_here / (denom_here + wiener_term)


def solution(mesh):
    in_specs = (
        P(("grp", "mem"), None),
        P(("grp", "mem")),
        P(("grp", "mem")),
        P(("grp", "mem")),
        P(),
    )
    out_specs = P("grp", "mem")
    return jax.shard_map(
        on_device, mesh=mesh, in_specs=in_specs, out_specs=out_specs, check_vma=False
    )
```

profile of v0, /device:TPU:4, one launch (start us, length us, event | category | flops | bytes accessed | tf_op | source)
XLA Modules:
  0.0 239.1 jit_solution(11630020243048273355)
XLA Ops:
  0.0 2.5 %copy.41 = bf16[4,8,8,2304]{3,2,0,1:T(8,128)(2,1)} copy(bf16[4,8,8,2304]{3,2,1,0:T(8,128)(2,1)} %bitcast.55) | data formatting | bytes 2359296 | tf_op jit(solution)/shard_map/all_to_all | solution.py:27
  2.5 4.9 %all-to-all-start = ((bf16[32,8,2304]{2,0,1:T(8,128)(2,1)}), bf16[32,8,2304]{2,0,1:T(8,128)(2,1)S(1)}, u32[]{:S(2)}, u32[]{:S(2)}) async-start(bf16[32,8,2304]{2,0,1:T(8,128)(2,1)} %bitcast.36), calls=%async_computation | async-start | bytes 2359296 | tf_op jit(solution)/shard_map/all_to_all | solution.py:27
  7.4 35.3 %all-gather = s32[8,32,3]{1,2,0:T(4,128)S(1)} all-gather(s32[1,32,3]{1,2,0:T(4,128)S(1)} %add_bitcast_fusion), channel_id=1, replica_groups=mesh['grp'=4,'mem'=8] {'mem'}, dimensions={0}, use_global_device_ids=true | all-gather | bytes 3456 | tf_op jit(solution)/shard_map/all_gather | solution.py:30
  43.5 4.3 %bitcast_multiply_fusion = (f32[256,2304]{1,0:T(8,128)}, f32[256,2304]{1,0:T(8,128)}, f32[256,2304]{1,0:T(8,128)}) fusion(bf16[32,8,2304]{2,0,1:T(8,128)(2,1)S(1)} %all-to-all-done, f32[16,18432]{1,0:T(8,128)S(1)} %copy-done, s32[]{:T(128)S(6)} %select_n.72, s32[256]{0:T(256)S(1)} %bitcast.58), kind=kOutput, calls=%fused_computation.12 | convolution fusion | flops 115019776 | bytes 8406020 | tf_op jit(solution)/shard_map/dot_general | solution.py:39
  51.5 3.0 %copy.32 = f32[256,2304]{0,1:T(8,128)} copy(f32[256,2304]{1,0:T(8,128)} %get-tuple-element.20) | data formatting | bytes 4718592 | tf_op jit(solution)/shard_map/mul | solution.py:42
  57.6 3.1 %broadcast_select_fusion.1 = (f32[256,16,144]{0,2,1:T(8,128)S(1)}, f32[256,16,144]{0,2,1:T(8,128)}, f32[256,16,144]{0,2,1:T(8,128)S(1)}, f32[256,16,144]{0,2,1:T(8,128)}) fusion(f32[256,16,144]{0,2,1:T(8,128)S(1)} %bitcast.39, pred[256]{0:T(512)(128)(4,1)S(1)} %copy-done.21, f32[256,16,4]{0,2,1:T(4,128)S(1)} %slice.112, f32[256,16,140]{0,2,1:T(8,128)S(1)} %copy-done.15, ...), kind=kLoop, calls=%fused_computation.41 | loop fusion | flops 2359296 | bytes 18874624 | tf_op jit(solution)/shard_map/jit(_where)/select_n | solution.py:22
  61.6 3.1 %pad_maximum_fusion.1 = (f32[256,16,144]{0,2,1:T(8,128)}, f32[256,16,144]{0,2,1:T(8,128)S(1)}, f32[256,16,144]{0,2,1:T(8,128)S(1)}, f32[256,16,144]{0,2,1:T(8,128)}) fusion(f32[256,16,8]{0,2,1:T(8,128)S(1)} %slice.114, f32[256,16,136]{0,2,1:T(8,128)S(1)} %slice.113, f32[256,16,144]{0,2,1:T(8,128)S(1)} %get-tuple-element.15, pred[256]{0:T(512)(128)(4,1)S(1)} %copy-done.20, ...), kind=kLoop, calls=%fused_computation.1 | loop fusion | flops 2359296 | bytes 18874624 | tf_op jit(solution)/shard_map/concatenate | solution.py:20
  80.9 3.1 %copy.30 = f32[256,2304]{1,0:T(8,128)} copy(f32[256,2304]{0,1:T(8,128)} %bitcast.53) | data formatting | bytes 4718592 | tf_op jit(solution)/shard_map/concatenate | solution.py:20
  84.0 3.2 %copy.29 = f32[256,2304]{1,0:T(8,128)} copy(f32[256,2304]{0,1:T(8,128)} %bitcast.51) | data formatting | bytes 4718592 | tf_op jit(solution)/shard_map/concatenate | solution.py:20
  89.2 3.2 %copy.27 = f32[256,2304]{1,0:T(8,128)} copy(f32[256,2304]{0,1:T(8,128)} %bitcast.48) | data formatting | bytes 4718592 | tf_op jit(solution)/shard_map/concatenate | solution.py:20
  92.4 2.0 copy.26
  96.2 2.0 copy.38
  98.2 3.2 %copy.37 = f32[256,2304]{1,0:T(8,128)} copy(f32[256,2304]{0,1:T(8,128)} %bitcast.54) | data formatting | bytes 4718592 | tf_op jit(solution)/shard_map/concatenate | solution.py:20
  103.4 3.2 %copy.35 = f32[256,2304]{1,0:T(8,128)} copy(f32[256,2304]{0,1:T(8,128)} %bitcast.50) | data formatting | bytes 4718592 | tf_op jit(solution)/shard_map/concatenate | solution.py:20
  108.6 3.2 %copy.33 = f32[256,2304]{1,0:T(8,128)} copy(f32[256,2304]{0,1:T(8,128)} %bitcast.45) | data formatting | bytes 4718592 | tf_op jit(solution)/shard_map/concatenate | solution.py:20
  111.9 8.5 %fusion.9 = f32[200,2304]{1,0:T(8,128)} fusion(f32[256,2304]{1,0:T(8,128)} %copy.31, f32[256,2304]{1,0:T(8,128)} %copy.30, f32[256,2304]{1,0:T(8,128)} %copy.29, f32[256,2304]{1,0:T(8,128)} %copy.28, f32[256,2304]{1,0:T(8,128)} %copy.27, f32[256,2304]{1,0:T(8,128)} %copy.26, f32[256,2304]{1,0:T(8,128)S(1)} %copy-done.3, pred[256]{0:T(512)(128)(4,1)S(1)} %copy-done.21, ...), kind=kOutput, calls=%fused_computation.20 | convolution fusion | flops 1419167744 | bytes 18360832 | tf_op jit(solution)/shard_map/dot_general | solution.py:41
  122.4 3.6 %fusion.2 = f32[200,2304]{1,0:T(8,128)} fusion(f32[256,2304]{1,0:T(8,128)S(1)} %copy-done.5, f32[256,2304]{1,0:T(8,128)S(1)} %copy-done.6, f32[256,2304]{1,0:T(8,128)S(1)} %copy-done.7, f32[256,2304]{1,0:T(8,128)S(1)} %copy-done.8, f32[256,2304]{1,0:T(8,128)S(1)} %copy-done.9, f32[256,2304]{1,0:T(8,128)S(1)} %copy-done.10, ...), kind=kOutput, calls=%fused_computation.13 | convolution fusion | flops 1419757568 | bytes 18360832 | tf_op jit(solution)/shard_map/dot_general | solution.py:43
  126.0 82.5 %fusion.36 = (f32[64,2304]{1,0:T(8,128)S(1)}, f32[64,2304]{1,0:T(8,128)S(1)}) fusion(f32[200,2304]{1,0:T(8,128)} %fusion.2, f32[200,2304]{1,0:T(8,128)S(1)} %copy-done.16), kind=kCustom, calls=%all-reduce-scatter.2 | all-reduce-scatter fusion | flops 1179649 | bytes 4866560
  208.5 2.7 %collective-permute-start = (f32[42,2304]{1,0:T(8,128)S(1)}, f32[42,2304]{1,0:T(8,128)}, u32[]{:S(2)}, u32[]{:S(2)}) collective-permute-start(f32[42,2304]{1,0:T(8,128)S(1)} %slice.135), channel_id=1, source_target_pairs={{0,8},{8,16},{16,24},{1,9},{9,17},{17,25},{2,10},{10,18},{18,26},{... | collective-permute-start | bytes 1161224
  211.3 2.1 collective-permute-start.1
  214.6 9.9 %collective-permute-done = f32[42,2304]{1,0:T(8,128)} collective-permute-done((f32[42,2304]{1,0:T(8,128)S(1)}, f32[42,2304]{1,0:T(8,128)}, u32[]{:S(2)}, u32[]{:S(2)}) %collective-permute-start) | collective-permute-done | bytes 387104
  224.5 3.2 %concatenate.84 = f32[106,2304]{1,0:T(8,128)S(1)} concatenate(f32[42,2304]{1,0:T(8,128)} %collective-permute-done, f32[64,2304]{1,0:T(8,128)} %copy-done.19), dimensions={0} | concatenate | bytes 1953792
  227.7 4.8 %collective-permute-done.1 = f32[42,2304]{1,0:T(8,128)} collective-permute-done((f32[42,2304]{1,0:T(8,128)S(1)}, f32[42,2304]{1,0:T(8,128)}, u32[]{:S(2)}, u32[]{:S(2)}) %collective-permute-start.1) | collective-permute-done | bytes 387104
  232.5 4.7 %concatenate.85 = f32[106,2304]{1,0:T(8,128)} concatenate(f32[42,2304]{1,0:T(8,128)} %collective-permute-done.1, f32[64,2304]{1,0:T(8,128)S(1)} %copy-done.18), dimensions={0} | concatenate | bytes 1953792
  (101 shorter events, 36.8 us)
Async XLA Ops:
  0.0 43.5 %copy-start = (f32[16,18432]{1,0:T(8,128)S(1)}, f32[16,18432]{1,0:T(8,128)}, u32[]{:S(2)}) copy-start(f32[16,18432]{1,0:T(8,128)} %param.9) | copy-start | bytes 3538948
  0.0 7.4 %copy-start.23 = (s32[32]{0:T(128)S(1)}, s32[32]{0:T(128)}, u32[]{:S(2)}) copy-start(s32[32]{0:T(128)} %param.7) | copy-start | bytes 388
  0.0 7.4 %copy-start.24 = (s32[32]{0:T(128)S(1)}, s32[32]{0:T(128)}, u32[]{:S(2)}) copy-start(s32[32]{0:T(128)} %param.8) | copy-start | bytes 388
  0.0 7.4 %copy-start.25 = (s32[32]{0:T(128)S(1)}, s32[32]{0:T(128)}, u32[]{:S(2)}) copy-start(s32[32]{0:T(128)} %param.6) | copy-start | bytes 388
  2.5 41.0 %all-to-all-start = ((bf16[32,8,2304]{2,0,1:T(8,128)(2,1)}), bf16[32,8,2304]{2,0,1:T(8,128)(2,1)S(1)}, u32[]{:S(2)}, u32[]{:S(2)}) async-start(bf16[32,8,2304]{2,0,1:T(8,128)(2,1)} %bitcast.36), calls=%async_computation | async-start | bytes 2359296 | tf_op jit(solution)/shard_map/all_to_all | solution.py:27
  84.0 3.2 %copy-start.13 = (f32[256,16,144]{0,2,1:T(8,128)S(1)}, f32[256,16,144]{0,2,1:T(8,128)}, u32[]{:S(2)}) copy-start(f32[256,16,144]{0,2,1:T(8,128)} %get-tuple-element.23) | copy-start | bytes 7077892
  89.2 3.2 %copy-start.11 = (f32[256,16,144]{0,2,1:T(8,128)S(1)}, f32[256,16,144]{0,2,1:T(8,128)}, u32[]{:S(2)}) copy-start(f32[256,16,144]{0,2,1:T(8,128)} %get-tuple-element.16) | copy-start | bytes 7077892
  98.2 3.2 %copy-start.14 = (f32[256,16,144]{0,2,1:T(8,128)S(1)}, f32[256,16,144]{0,2,1:T(8,128)}, u32[]{:S(2)}) copy-start(f32[256,16,144]{0,2,1:T(8,128)} %get-tuple-element.33) | copy-start | bytes 7077892
  103.4 3.2 %copy-start.12 = (f32[256,16,144]{0,2,1:T(8,128)S(1)}, f32[256,16,144]{0,2,1:T(8,128)}, u32[]{:S(2)}) copy-start(f32[256,16,144]{0,2,1:T(8,128)} %get-tuple-element.43) | copy-start | bytes 7077892
  108.6 3.2 %copy-start.3 = (f32[256,2304]{1,0:T(8,128)S(1)}, f32[256,2304]{1,0:T(8,128)}, u32[]{:S(2)}) copy-start(f32[256,2304]{1,0:T(8,128)} %get-tuple-element.19) | copy-start | bytes 7077892
  108.6 3.2 %copy-start.22 = (pred[256]{0:T(512)(128)(4,1)S(1)}, pred[256]{0:T(512)(128)(4,1)}, u32[]{:S(2)}) copy-start(pred[256]{0:T(512)(128)(4,1)} %get-tuple-element.5) | copy-start | bytes 772
  111.8 8.6 %copy-start.4 = (f32[256,2304]{1,0:T(8,128)S(1)}, f32[256,2304]{1,0:T(8,128)}, u32[]{:S(2)}) copy-start(f32[256,2304]{1,0:T(8,128)} %get-tuple-element.41) | copy-start | bytes 7077892
  111.9 8.6 %copy-start.5 = (f32[256,2304]{1,0:T(8,128)S(1)}, f32[256,2304]{1,0:T(8,128)}, u32[]{:S(2)}) copy-start(f32[256,2304]{1,0:T(8,128)} %copy.38) | copy-start | bytes 7077892
  111.9 8.6 %copy-start.6 = (f32[256,2304]{1,0:T(8,128)S(1)}, f32[256,2304]{1,0:T(8,128)}, u32[]{:S(2)}) copy-start(f32[256,2304]{1,0:T(8,128)} %copy.37) | copy-start | bytes 7077892
  111.9 8.6 %copy-start.7 = (f32[256,2304]{1,0:T(8,128)S(1)}, f32[256,2304]{1,0:T(8,128)}, u32[]{:S(2)}) copy-start(f32[256,2304]{1,0:T(8,128)} %copy.36) | copy-start | bytes 7077892
  111.9 8.9 %copy-start.8 = (f32[256,2304]{1,0:T(8,128)S(1)}, f32[256,2304]{1,0:T(8,128)}, u32[]{:S(2)}) copy-start(f32[256,2304]{1,0:T(8,128)} %copy.35) | copy-start | bytes 7077892
  111.9 9.8 %copy-start.9 = (f32[256,2304]{1,0:T(8,128)S(1)}, f32[256,2304]{1,0:T(8,128)}, u32[]{:S(2)}) copy-start(f32[256,2304]{1,0:T(8,128)} %copy.34) | copy-start | bytes 7077892
  111.9 10.5 %copy-start.10 = (f32[256,2304]{1,0:T(8,128)S(1)}, f32[256,2304]{1,0:T(8,128)}, u32[]{:S(2)}) copy-start(f32[256,2304]{1,0:T(8,128)} %copy.33) | copy-start | bytes 7077892
  122.4 3.6 %copy-start.16 = (f32[200,2304]{1,0:T(8,128)S(1)}, f32[200,2304]{1,0:T(8,128)}, u32[]{:S(2)}) copy-start(f32[200,2304]{1,0:T(8,128)} %fusion.9) | copy-start | bytes 5529604
  126.0 87.4 %copy-start.26 = (u32[32]{0:T(128)S(1)}, u32[32]{0:T(128)}, u32[]{:S(2)}) copy-start(u32[32]{0:T(128)} %constant.25) | copy-start | bytes 388
  208.5 16.0 %collective-permute-start = (f32[42,2304]{1,0:T(8,128)S(1)}, f32[42,2304]{1,0:T(8,128)}, u32[]{:S(2)}, u32[]{:S(2)}) collective-permute-start(f32[42,2304]{1,0:T(8,128)S(1)} %slice.135), channel_id=1, source_target_pairs={{0,8},{8,16},{16,24},{1,9},{9,17},{17,25},{2,10},{10,18},{18,26},{... | collective-permute-start | bytes 1161224
  211.3 21.2 %copy-start.18 = (f32[64,2304]{1,0:T(8,128)S(1)}, f32[64,2304]{1,0:T(8,128)}, u32[]{:S(2)}) copy-start(f32[64,2304]{1,0:T(8,128)} %copy-done.17) | copy-start | bytes 1769476
  211.3 21.2 %collective-permute-start.1 = (f32[42,2304]{1,0:T(8,128)S(1)}, f32[42,2304]{1,0:T(8,128)}, u32[]{:S(2)}, u32[]{:S(2)}) collective-permute-start(f32[42,2304]{1,0:T(8,128)S(1)} %slice.136), channel_id=1, source_target_pairs={{0,8},{8,16},{16,24},{1,9},{9,17},{17,25},{2,10},{10,18},{18,26},{... | collective-permute-start | bytes 1161224
  214.6 24.6 %copy-start.1 = (f32[16,18432]{1,0:T(8,128)S(1)}, f32[16,18432]{1,0:T(8,128)}, u32[]{:S(2)}) copy-start(f32[16,18432]{1,0:T(8,128)} %param.9) | copy-start | bytes 3538948
  (6 other events, 14.7 us)
where the time goes:
time: 240 us; the launch traced here: 239 us
  blocking collectives  118 us (49%)
  local copies, waits for them, and re-layouts  57.7 us (24%)
  other arithmetic  21.9 us (9%)
  matrix products  16.4 us (7%)
  waiting for transfers between devices  14.7 us (6%)
  starting transfers between devices  9.6 us (4%)
    unnamed x1, blocking collectives  82.5 us
    all_gather x1, blocking collectives, on_device(): tags = lax.all_gather(labels, 'mem', axis=0, tiled=True)  35.3 us
    concatenate x12, local copies, waits for them, and re-layouts, rotate(): jnp.concatenate([shaped[:, :, amount:], shaped[:, :, :amount]], axis=2)  31.1 us
    concatenate x9, other arithmetic, rotate(): jnp.concatenate([shaped[:, :, amount:], shaped[:, :, :amount]], axis=2)  16.2 us
    unnamed x2, waiting for transfers between devices  14.7 us
    unnamed x60, local copies, waits for them, and re-layouts  12.1 us
    dot_general x1, matrix products, on_device(): numer = jnp.dot(member, aligned, precision=lax.Precision.HIGHEST)  8.54 us
    slice x12, local copies, waits for them, and re-layouts, rotate(): shaped[:, :, amount:]  4.89 us
  transfers between devices with their start and end apart: 3, of which 2 were waited for; matrix products, arithmetic and copies ran while one was open for 2% of the time, Pallas kernels for 0%

commit v1 on v0

--- a/solution.py
+++ b/solution.py
@@ -27,7 +27,12 @@
     arrived = lax.all_to_all(images, "mem", split_axis=1, concat_axis=0, tiled=True)
     span = arrived.shape[1]
     labels = jnp.stack([classes, bins, rotations], axis=1)
-    tags = lax.all_gather(labels, "mem", axis=0, tiled=True)
+    ring = [labels]
+    for hop in range(7):
+        ring.append(lax.ppermute(ring[-1], "mem", [(dev, (dev + 1) % 8) for dev in range(8)]))
+    tags = jnp.roll(
+        jnp.concatenate(ring[::-1], axis=0), (lax.axis_index("mem") + 1) * ring[0].shape[0], axis=0
+    )
     class_here = tags[:, 0]
     bin_here = tags[:, 1]
     turn_here = tags[:, 2]

time: 240 us -> 249 us (1.038)
  waiting for transfers between devices: 14.7 us -> 62.6 us
  blocking collectives: 118 us -> 78.5 us
    ppermute x0 -> x7, waiting for transfers between devices: none -> 52 us  [on_device(): lax.ppermute(ring[-1], 'mem', [(dev, (dev + 1) % 8) for dev in range(8)])]
    all_gather x1 -> x0, blocking collectives: 35.3 us -> none  [on_device(): tags = lax.all_gather(labels, 'mem', axis=0, tiled=True)]
    unnamed x2, waiting for transfers between devices: 14.7 us -> 10.6 us
    unnamed x1, blocking collectives: 82.5 us -> 78.5 us
    unnamed x60 -> x59, local copies, waits for them, and re-layouts: 12.1 us -> 12 us
  transfers between devices with their start and end apart: 3 -> 10, of which waited for: 2 -> 9; matrix products, arithmetic and copies ran while one was open for 2% -> 2% of each run, Pallas kernels for 0% -> 0%
where the time goes in v1:
time: 249 us; the launch traced here: 248 us
  blocking collectives  78.5 us (32%)
  waiting for transfers between devices  62.6 us (25%)
  local copies, waits for them, and re-layouts  57.8 us (23%)
  other arithmetic  21.8 us (9%)
  matrix products  16.3 us (7%)
  starting transfers between devices  10.2 us (4%)
    unnamed x1, blocking collectives  78.5 us
    ppermute x7, waiting for transfers between devices, on_device(): lax.ppermute(ring[-1], 'mem', [(dev, (dev + 1) % 8) for dev in range(8)])  52 us
    concatenate x12, local copies, waits for them, and re-layouts, rotate(): jnp.concatenate([shaped[:, :, amount:], shaped[:, :, :amount]], axis=2)  31.1 us
    concatenate x9, other arithmetic, rotate(): jnp.concatenate([shaped[:, :, amount:], shaped[:, :, :amount]], axis=2)  16.2 us
    unnamed x59, local copies, waits for them, and re-layouts  12 us
    unnamed x2, waiting for transfers between devices  10.6 us
    dot_general x1, matrix products, on_device(): numer = jnp.dot(member, aligned, precision=lax.Precision.HIGHEST)  8.54 us
  transfers between devices with their start and end apart: 10, of which 9 were waited for; matrix products, arithmetic and copies ran while one was open for 2% of the time, Pallas kernels for 0%

profile of v1, /device:TPU:4, one launch (start us, length us, event | category | flops | bytes accessed | tf_op | source)
XLA Modules:
  0.0 248.3 jit_solution(5755214173676745593)
XLA Ops:
  2.5 4.9 %all-to-all-start = ((bf16[32,8,2304]{2,0,1:T(8,128)(2,1)}), bf16[32,8,2304]{2,0,1:T(8,128)(2,1)S(1)}, u32[]{:S(2)}, u32[]{:S(2)}) async-start(bf16[32,8,2304]{2,0,1:T(8,128)(2,1)} %bitcast.32), calls=%async_computation | async-start | bytes 2359296 | tf_op jit(solution)/shard_map/all_to_all | solution.py:27
  8.0 23.1 %collective-permute-done = s32[32,3]{0,1:T(4,128)S(1)} collective-permute-done((s32[32,3]{0,1:T(4,128)S(1)}, s32[32,3]{0,1:T(4,128)S(1)}, u32[]{:S(2)}, u32[]{:S(2)}) %collective-permute-start) | collective-permute-done | bytes 416 | tf_op jit(solution)/shard_map/ppermute | solution.py:32
  31.1 4.9 %collective-permute-done.1 = s32[32,3]{0,1:T(4,128)S(1)} collective-permute-done((s32[32,3]{0,1:T(4,128)S(1)}, s32[32,3]{0,1:T(4,128)S(1)}, u32[]{:S(2)}, u32[]{:S(2)}) %collective-permute-start.1) | collective-permute-done | bytes 416 | tf_op jit(solution)/shard_map/ppermute | solution.py:32
  36.0 4.8 %collective-permute-done.2 = s32[32,3]{0,1:T(4,128)S(1)} collective-permute-done((s32[32,3]{0,1:T(4,128)S(1)}, s32[32,3]{0,1:T(4,128)S(1)}, u32[]{:S(2)}, u32[]{:S(2)}) %collective-permute-start.2) | collective-permute-done | bytes 416 | tf_op jit(solution)/shard_map/ppermute | solution.py:32
  40.8 4.8 %collective-permute-done.3 = s32[32,3]{0,1:T(4,128)S(1)} collective-permute-done((s32[32,3]{0,1:T(4,128)S(1)}, s32[32,3]{0,1:T(4,128)S(1)}, u32[]{:S(2)}, u32[]{:S(2)}) %collective-permute-start.3) | collective-permute-done | bytes 416 | tf_op jit(solution)/shard_map/ppermute | solution.py:32
  45.6 4.8 %collective-permute-done.4 = s32[32,3]{0,1:T(4,128)S(1)} collective-permute-done((s32[32,3]{0,1:T(4,128)S(1)}, s32[32,3]{0,1:T(4,128)S(1)}, u32[]{:S(2)}, u32[]{:S(2)}) %collective-permute-start.4) | collective-permute-done | bytes 416 | tf_op jit(solution)/shard_map/ppermute | solution.py:32
  50.4 4.8 %collective-permute-done.5 = s32[32,3]{0,1:T(4,128)S(1)} collective-permute-done((s32[32,3]{0,1:T(4,128)S(1)}, s32[32,3]{0,1:T(4,128)S(1)}, u32[]{:S(2)}, u32[]{:S(2)}) %collective-permute-start.5) | collective-permute-done | bytes 416 | tf_op jit(solution)/shard_map/ppermute | solution.py:32
  55.2 4.8 %collective-permute-done.6 = s32[32,3]{0,1:T(4,128)S(1)} collective-permute-done((s32[32,3]{0,1:T(4,128)S(1)}, s32[32,3]{0,1:T(4,128)S(1)}, u32[]{:S(2)}, u32[]{:S(2)}) %collective-permute-start.6) | collective-permute-done | bytes 416 | tf_op jit(solution)/shard_map/ppermute | solution.py:32
  60.8 4.2 %bitcast_multiply_fusion = (f32[256,2304]{1,0:T(8,128)}, f32[256,2304]{1,0:T(8,128)}, f32[256,2304]{1,0:T(8,128)}) fusion(bf16[32,8,2304]{2,0,1:T(8,128)(2,1)S(1)} %all-to-all-done, f32[16,18432]{1,0:T(8,128)S(1)} %copy-done, s32[]{:T(128)S(6)} %select_n.87, s32[256]{0:T(256)S(1)} %bitcast.54), kind=kOutput, calls=%fused_computation.12 | convolution fusion | flops 115019776 | bytes 8406020 | tf_op jit(solution)/shard_map/dot_general | solution.py:44
  68.8 3.1 %copy.30 = f32[256,2304]{0,1:T(8,128)} copy(f32[256,2304]{1,0:T(8,128)} %get-tuple-element.20) | data formatting | bytes 4718592 | tf_op jit(solution)/shard_map/mul | solution.py:47
  74.9 3.1 %broadcast_select_fusion.1 = (f32[256,16,144]{0,2,1:T(8,128)S(1)}, f32[256,16,144]{0,2,1:T(8,128)}, f32[256,16,144]{0,2,1:T(8,128)S(1)}, f32[256,16,144]{0,2,1:T(8,128)}) fusion(f32[256,16,144]{0,2,1:T(8,128)S(1)} %bitcast.35, pred[256]{0:T(512)(128)(4,1)S(1)} %copy-done.20, f32[256,16,4]{0,2,1:T(4,128)S(1)} %slice.109, f32[256,16,140]{0,2,1:T(8,128)S(1)} %copy-done.15, ...), kind=kLoop, calls=%fused_computation.41 | loop fusion | flops 2359296 | bytes 18874624 | tf_op jit(solution)/shard_map/jit(_where)/select_n | solution.py:22
  78.8 3.1 %pad_maximum_fusion.1 = (f32[256,16,144]{0,2,1:T(8,128)}, f32[256,16,144]{0,2,1:T(8,128)S(1)}, f32[256,16,144]{0,2,1:T(8,128)S(1)}, f32[256,16,144]{0,2,1:T(8,128)}) fusion(f32[256,16,8]{0,2,1:T(8,128)S(1)} %slice.111, f32[256,16,136]{0,2,1:T(8,128)S(1)} %slice.110, f32[256,16,144]{0,2,1:T(8,128)S(1)} %get-tuple-element.15, pred[256]{0:T(512)(128)(4,1)S(1)} %copy-done.21, ...), kind=kLoop, calls=%fused_computation.1 | loop fusion | flops 2359296 | bytes 18874624 | tf_op jit(solution)/shard_map/concatenate | solution.py:20
  98.1 3.1 %copy.28 = f32[256,2304]{1,0:T(8,128)} copy(f32[256,2304]{0,1:T(8,128)} %bitcast.49) | data formatting | bytes 4718592 | tf_op jit(solution)/shard_map/concatenate | solution.py:20
  101.2 3.2 %copy.27 = f32[256,2304]{1,0:T(8,128)} copy(f32[256,2304]{0,1:T(8,128)} %bitcast.47) | data formatting | bytes 4718592 | tf_op jit(solution)/shard_map/concatenate | solution.py:20
  106.4 3.2 %copy.25 = f32[256,2304]{1,0:T(8,128)} copy(f32[256,2304]{0,1:T(8,128)} %bitcast.44) | data formatting | bytes 4718592 | tf_op jit(solution)/shard_map/concatenate | solution.py:20
  115.4 3.2 %copy.35 = f32[256,2304]{1,0:T(8,128)} copy(f32[256,2304]{0,1:T(8,128)} %bitcast.50) | data formatting | bytes 4718592 | tf_op jit(solution)/shard_map/concatenate | solution.py:20
  120.6 3.2 %copy.33 = f32[256,2304]{1,0:T(8,128)} copy(f32[256,2304]{0,1:T(8,128)} %bitcast.46) | data formatting | bytes 4718592 | tf_op jit(solution)/shard_map/concatenate | solution.py:20
  125.8 3.2 %copy.31 = f32[256,2304]{1,0:T(8,128)} copy(f32[256,2304]{0,1:T(8,128)} %bitcast.41) | data formatting | bytes 4718592 | tf_op jit(solution)/shard_map/concatenate | solution.py:20
  129.1 8.5 %fusion.9 = f32[200,2304]{1,0:T(8,128)} fusion(f32[256,2304]{1,0:T(8,128)} %copy.29, f32[256,2304]{1,0:T(8,128)} %copy.28, f32[256,2304]{1,0:T(8,128)} %copy.27, f32[256,2304]{1,0:T(8,128)} %copy.26, f32[256,2304]{1,0:T(8,128)} %copy.25, f32[256,2304]{1,0:T(8,128)} %copy.24, f32[256,2304]{1,0:T(8,128)S(1)} %copy-done.3, pred[256]{0:T(512)(128)(4,1)S(1)} %copy-done.20, ...), kind=kOutput, calls=%fused_computation.20 | convolution fusion | flops 1419167744 | bytes 18360832 | tf_op jit(solution)/shard_map/dot_general | solution.py:46
  139.6 3.5 %fusion.2 = f32[200,2304]{1,0:T(8,128)} fusion(f32[256,2304]{1,0:T(8,128)S(1)} %copy-done.5, f32[256,2304]{1,0:T(8,128)S(1)} %copy-done.6, f32[256,2304]{1,0:T(8,128)S(1)} %copy-done.7, f32[256,2304]{1,0:T(8,128)S(1)} %copy-done.8, f32[256,2304]{1,0:T(8,128)S(1)} %copy-done.9, f32[256,2304]{1,0:T(8,128)S(1)} %copy-done.10, ...), kind=kOutput, calls=%fused_computation.13 | convolution fusion | flops 1419757568 | bytes 18360832 | tf_op jit(solution)/shard_map/dot_general | solution.py:48
  143.2 78.5 %fusion.36 = (f32[64,2304]{1,0:T(8,128)S(1)}, f32[64,2304]{1,0:T(8,128)S(1)}) fusion(f32[200,2304]{1,0:T(8,128)} %fusion.2, f32[200,2304]{1,0:T(8,128)S(1)} %copy-done.16), kind=kCustom, calls=%all-reduce-scatter.2 | all-reduce-scatter fusion | flops 1179649 | bytes 4866560
  227.8 9.1 %collective-permute-done.7 = f32[42,2304]{1,0:T(8,128)} collective-permute-done((f32[42,2304]{1,0:T(8,128)S(1)}, f32[42,2304]{1,0:T(8,128)}, u32[]{:S(2)}, u32[]{:S(2)}) %collective-permute-start.7) | collective-permute-done | bytes 387104
  236.9 3.2 %concatenate.91 = f32[106,2304]{1,0:T(8,128)S(1)} concatenate(f32[42,2304]{1,0:T(8,128)} %collective-permute-done.7, f32[64,2304]{1,0:T(8,128)} %copy-done.19), dimensions={0} | concatenate | bytes 1953792
  241.6 4.7 %concatenate.92 = f32[106,2304]{1,0:T(8,128)} concatenate(f32[42,2304]{1,0:T(8,128)} %collective-permute-done.8, f32[64,2304]{1,0:T(8,128)S(1)} %copy-done.18), dimensions={0} | concatenate | bytes 1953792
  (113 shorter events, 50.2 us)
Async XLA Ops:
  0.0 60.8 %copy-start = (f32[16,18432]{1,0:T(8,128)S(1)}, f32[16,18432]{1,0:T(8,128)}, u32[]{:S(2)}) copy-start(f32[16,18432]{1,0:T(8,128)} %param.9) | copy-start | bytes 3538948
  0.0 7.4 %copy-start.23 = (s32[32]{0:T(128)S(1)}, s32[32]{0:T(128)}, u32[]{:S(2)}) copy-start(s32[32]{0:T(128)} %param.7) | copy-start | bytes 388
  0.0 7.4 %copy-start.24 = (s32[32]{0:T(128)S(1)}, s32[32]{0:T(128)}, u32[]{:S(2)}) copy-start(s32[32]{0:T(128)} %param.8) | copy-start | bytes 388
  0.0 7.4 %copy-start.25 = (s32[32]{0:T(128)S(1)}, s32[32]{0:T(128)}, u32[]{:S(2)}) copy-start(s32[32]{0:T(128)} %param.6) | copy-start | bytes 388
  2.5 58.3 %all-to-all-start = ((bf16[32,8,2304]{2,0,1:T(8,128)(2,1)}), bf16[32,8,2304]{2,0,1:T(8,128)(2,1)S(1)}, u32[]{:S(2)}, u32[]{:S(2)}) async-start(bf16[32,8,2304]{2,0,1:T(8,128)(2,1)} %bitcast.32), calls=%async_computation | async-start | bytes 2359296 | tf_op jit(solution)/shard_map/all_to_all | solution.py:27
  7.4 23.6 %collective-permute-start = (s32[32,3]{0,1:T(4,128)S(1)}, s32[32,3]{0,1:T(4,128)S(1)}, u32[]{:S(2)}, u32[]{:S(2)}) collective-permute-start(s32[32,3]{0,1:T(4,128)S(1)} %pad_add_fusion), channel_id=1, source_target_pairs={{0,1},{1,2},{2,3},{3,4},{4,5},{5,6},{6,7},{7,0},{8,9},{9,10},{10,1... | collective-permute-start | bytes 1160 | tf_op jit(solution)/shard_map/ppermute | solution.py:32
  31.1 4.9 %collective-permute-start.1 = (s32[32,3]{0,1:T(4,128)S(1)}, s32[32,3]{0,1:T(4,128)S(1)}, u32[]{:S(2)}, u32[]{:S(2)}) collective-permute-start(s32[32,3]{0,1:T(4,128)S(1)} %collective-permute-done), channel_id=1, source_target_pairs={{0,1},{1,2},{2,3},{3,4},{4,5},{5,6},{6,7},{7,0},{8,9},{9,10},{10,1... | collective-permute-start | bytes 1160 | tf_op jit(solution)/shard_map/ppermute | solution.py:32
  36.0 4.8 %collective-permute-start.2 = (s32[32,3]{0,1:T(4,128)S(1)}, s32[32,3]{0,1:T(4,128)S(1)}, u32[]{:S(2)}, u32[]{:S(2)}) collective-permute-start(s32[32,3]{0,1:T(4,128)S(1)} %collective-permute-done.1), channel_id=1, source_target_pairs={{0,1},{1,2},{2,3},{3,4},{4,5},{5,6},{6,7},{7,0},{8,9},{9,10},{10,1... | collective-permute-start | bytes 1160 | tf_op jit(solution)/shard_map/ppermute | solution.py:32
  40.8 4.8 %collective-permute-start.3 = (s32[32,3]{0,1:T(4,128)S(1)}, s32[32,3]{0,1:T(4,128)S(1)}, u32[]{:S(2)}, u32[]{:S(2)}) collective-permute-start(s32[32,3]{0,1:T(4,128)S(1)} %collective-permute-done.2), channel_id=1, source_target_pairs={{0,1},{1,2},{2,3},{3,4},{4,5},{5,6},{6,7},{7,0},{8,9},{9,10},{10,1... | collective-permute-start | bytes 1160 | tf_op jit(solution)/shard_map/ppermute | solution.py:32
  45.6 4.8 %collective-permute-start.4 = (s32[32,3]{0,1:T(4,128)S(1)}, s32[32,3]{0,1:T(4,128)S(1)}, u32[]{:S(2)}, u32[]{:S(2)}) collective-permute-start(s32[32,3]{0,1:T(4,128)S(1)} %collective-permute-done.3), channel_id=1, source_target_pairs={{0,1},{1,2},{2,3},{3,4},{4,5},{5,6},{6,7},{7,0},{8,9},{9,10},{10,1... | collective-permute-start | bytes 1160 | tf_op jit(solution)/shard_map/ppermute | solution.py:32
  50.4 4.8 %collective-permute-start.5 = (s32[32,3]{0,1:T(4,128)S(1)}, s32[32,3]{0,1:T(4,128)S(1)}, u32[]{:S(2)}, u32[]{:S(2)}) collective-permute-start(s32[32,3]{0,1:T(4,128)S(1)} %collective-permute-done.4), channel_id=1, source_target_pairs={{0,1},{1,2},{2,3},{3,4},{4,5},{5,6},{6,7},{7,0},{8,9},{9,10},{10,1... | collective-permute-start | bytes 1160 | tf_op jit(solution)/shard_map/ppermute | solution.py:32
  55.2 4.8 %collective-permute-start.6 = (s32[32,3]{0,1:T(4,128)S(1)}, s32[32,3]{0,1:T(4,128)S(1)}, u32[]{:S(2)}, u32[]{:S(2)}) collective-permute-start(s32[32,3]{0,1:T(4,128)S(1)} %collective-permute-done.5), channel_id=1, source_target_pairs={{0,1},{1,2},{2,3},{3,4},{4,5},{5,6},{6,7},{7,0},{8,9},{9,10},{10,1... | collective-permute-start | bytes 1160 | tf_op jit(solution)/shard_map/ppermute | solution.py:32
  129.1 8.6 %copy-start.4 = (f32[256,2304]{1,0:T(8,128)S(1)}, f32[256,2304]{1,0:T(8,128)}, u32[]{:S(2)}) copy-start(f32[256,2304]{1,0:T(8,128)} %get-tuple-element.42) | copy-start | bytes 7077892
  129.1 8.6 %copy-start.5 = (f32[256,2304]{1,0:T(8,128)S(1)}, f32[256,2304]{1,0:T(8,128)}, u32[]{:S(2)}) copy-start(f32[256,2304]{1,0:T(8,128)} %copy.36) | copy-start | bytes 7077892
  129.1 8.6 %copy-start.6 = (f32[256,2304]{1,0:T(8,128)S(1)}, f32[256,2304]{1,0:T(8,128)}, u32[]{:S(2)}) copy-start(f32[256,2304]{1,0:T(8,128)} %copy.35) | copy-start | bytes 7077892
  129.1 8.6 %copy-start.7 = (f32[256,2304]{1,0:T(8,128)S(1)}, f32[256,2304]{1,0:T(8,128)}, u32[]{:S(2)}) copy-start(f32[256,2304]{1,0:T(8,128)} %copy.34) | copy-start | bytes 7077892
  129.1 8.9 %copy-start.8 = (f32[256,2304]{1,0:T(8,128)S(1)}, f32[256,2304]{1,0:T(8,128)}, u32[]{:S(2)}) copy-start(f32[256,2304]{1,0:T(8,128)} %copy.33) | copy-start | bytes 7077892
  129.1 9.8 %copy-start.9 = (f32[256,2304]{1,0:T(8,128)S(1)}, f32[256,2304]{1,0:T(8,128)}, u32[]{:S(2)}) copy-start(f32[256,2304]{1,0:T(8,128)} %copy.32) | copy-start | bytes 7077892
  129.1 10.5 %copy-start.10 = (f32[256,2304]{1,0:T(8,128)S(1)}, f32[256,2304]{1,0:T(8,128)}, u32[]{:S(2)}) copy-start(f32[256,2304]{1,0:T(8,128)} %copy.31) | copy-start | bytes 7077892
  143.2 83.4 %copy-start.26 = (u32[32]{0:T(128)S(1)}, u32[32]{0:T(128)}, u32[]{:S(2)}) copy-start(u32[32]{0:T(128)} %constant.49) | copy-start | bytes 388
  221.8 15.1 %collective-permute-start.7 = (f32[42,2304]{1,0:T(8,128)S(1)}, f32[42,2304]{1,0:T(8,128)}, u32[]{:S(2)}, u32[]{:S(2)}) collective-permute-start(f32[42,2304]{1,0:T(8,128)S(1)} %slice.132), channel_id=1, source_target_pairs={{0,8},{8,16},{16,24},{1,9},{9,17},{17,25},{2,10},{10,18},{18,26},{... | collective-permute-start | bytes 1161224
  224.5 17.1 %copy-start.18 = (f32[64,2304]{1,0:T(8,128)S(1)}, f32[64,2304]{1,0:T(8,128)}, u32[]{:S(2)}) copy-start(f32[64,2304]{1,0:T(8,128)} %copy-done.17) | copy-start | bytes 1769476
  224.5 17.1 %collective-permute-start.8 = (f32[42,2304]{1,0:T(8,128)S(1)}, f32[42,2304]{1,0:T(8,128)}, u32[]{:S(2)}, u32[]{:S(2)}) collective-permute-start(f32[42,2304]{1,0:T(8,128)S(1)} %slice.133), channel_id=1, source_target_pairs={{0,8},{8,16},{16,24},{1,9},{9,17},{17,25},{2,10},{10,18},{18,26},{... | collective-permute-start | bytes 1161224
  227.8 20.5 %copy-start.1 = (f32[16,18432]{1,0:T(8,128)S(1)}, f32[16,18432]{1,0:T(8,128)}, u32[]{:S(2)}) copy-start(f32[16,18432]{1,0:T(8,128)} %param.9) | copy-start | bytes 3538948
  (13 other events, 37.5 us)
